TPU v7x, 32 devices: a whole 2x2x4 slice. The times are simulated.
32 devices in a mesh: dp: 4 (over y, core), tensor: 8 (over z, x).
Axes of the slice: x: 2, y: 2, z: 4, core: 2. Of those that a mesh axis runs over, the one named last changes fastest.
Arguments:
- token_ids: int32 [1024], P('dp'), may hold values from 0 to 128255
- attn_heads: bfloat16 [1024, 8192], P('dp', 'tensor'), may hold values from -6 to 6
- out_proj: bfloat16 [8192, 8192], P('tensor'), may hold values from -0.0625 to 0.0625
- residual: bfloat16 [1024, 8192], P(('dp', 'tensor')), may hold values from -6 to 6
- norm_gain: float32 [8192], replicated, may hold values from 0.5 to 1.5
- twist_in: bfloat16 [8192, 8192], P('dp', 'tensor'), may hold values from -0.0625 to 0.0625
- twist_out: float32 [8192], P('tensor'), may hold values from -0.26516503 to 0.26516503
- token_bias: float32 [128256], replicated, may hold values from -4 to 262
- toxicity: int32 [4], P('dp'), may hold values from 1 to 4
- prompt_len: int32 [4], P('dp'), may hold values from 1 to 128
Outputs:
- twist_vals: float32 [1024], P('dp')
- grad_in: float32 [8192, 8192], P('dp', 'tensor')
- grad_out: float32 [8192], P('tensor')
- grad_bias: float32 [128256], P('dp')
All inputs are finite; a program needn't handle non-finite values.
Results may differ from a plain program's by a relative error of at most 0.033.
Values may be sent and summed in bfloat16 or wider, within the bound.
A program may use at most 128 MiB of HBM per device.

v0:
```python
import jax
import jax.numpy as jnp
from jax import lax
from jax.sharding import PartitionSpec as P


def merged_2(value, axis, join):
    pieces = jax.tree.map(lambda part: lax.all_gather(part, axis), value)
    head = jax.tree.map(lambda part: part[0], pieces)
    tail = jax.tree.map(lambda part: part[1:], pieces)
    total, _ = lax.scan(lambda total, share: (join(total, share), None), head, tail)
    return total


def normalize(hidden, norm_gain):
    values = hidden.astype(jnp.float32)
    scaled = lax.rsqrt(jnp.mean(values * values, axis=-1, keepdims=True) + 1e-05)
    return (values * scaled * norm_gain[None, :]).astype(jnp.bfloat16)


def combine(earlier, later):
    high_one, sum_one, lab_one = earlier
    high_two, sum_two, lab_two = later
    highest = jnp.maximum(high_one, high_two)
    merged = sum_one * jnp.exp(high_one - highest) + sum_two * jnp.exp(high_two - highest)
    return (highest, merged, lab_one + lab_two)


def local(
    token_ids,
    attn_heads,
    out_proj,
    residual,
    norm_gain,
    twist_in,
    twist_out,
    token_bias,
    toxicity,
    prompt_len,
):
    seq_len = attn_heads.shape[0]
    vocab_size = token_bias.shape[0]
    partial_sum = jnp.dot(attn_heads, out_proj, preferred_element_type=jnp.float32)
    summed = lax.psum(partial_sum.astype(jnp.bfloat16), "tensor").astype(jnp.float32)
    resid_all = lax.all_gather(residual, "tensor", axis=0, tiled=True)
    hidden = (resid_all.astype(jnp.float32) + summed).astype(jnp.bfloat16)
    normed = normalize(hidden, norm_gain)
    columns = normed
    pre_act = jnp.dot(
        columns,
        lax.all_gather(twist_in, "dp", axis=0, tiled=True),
        preferred_element_type=jnp.float32,
    )
    active = jax.nn.silu(pre_act)
    partial_psi = jnp.dot(active, twist_out, precision=lax.Precision.HIGHEST)
    twist_vals = lax.psum(partial_psi, "tensor") + token_bias[token_ids]
    live = jnp.arange(seq_len) >= prompt_len[0]
    live_float = live.astype(jnp.float32)
    levels = toxicity[0].astype(jnp.float32) * live_float
    local_high = jnp.where(live, twist_vals, -1e30)
    highest, totals, lab_sum = merged_2((local_high, live_float, levels), "dp", combine)
    expo = jnp.where(live, jnp.exp(jnp.where(live, twist_vals - highest, -80.0)), 0.0)
    weights = (expo / jnp.maximum(totals, 1.0) - levels / jnp.maximum(lab_sum, 1.0)) / seq_len
    grad_out = lax.psum(jnp.dot(weights, active, precision=lax.Precision.HIGHEST), "dp")
    local_bias = jnp.zeros((vocab_size,), jnp.float32).at[token_ids].add(weights)
    grad_bias = lax.psum_scatter(
        local_bias.astype(jnp.bfloat16), "dp", scatter_dimension=0, tiled=True
    ).astype(jnp.float32)
    sigma = jax.nn.sigmoid(pre_act)
    d_pre = (
        weights[:, None] * twist_out[None, :] * sigma * (1.0 + pre_act * (1.0 - sigma))
    ).astype(jnp.bfloat16)
    contract = (((0,), (0,)), ((), ()))
    columns = normed
    grad_in = lax.psum_scatter(
        lax.dot_general(columns, d_pre, contract, preferred_element_type=jnp.float32).astype(
            jnp.bfloat16
        ),
        "dp",
        scatter_dimension=0,
        tiled=True,
    ).astype(jnp.float32)
    return (twist_vals, grad_in, grad_out, grad_bias)


def solution(mesh):
    placed = (
        P("dp"),
        P("dp", "tensor"),
        P("tensor", None),
        P(("dp", "tensor"), None),
        P(),
        P("dp", "tensor"),
        P("tensor"),
        P(),
        P("dp"),
        P("dp"),
    )
    return jax.shard_map(
        local,
        mesh=mesh,
        in_specs=placed,
        out_specs=(P("dp"), P("dp", "tensor"), P("tensor"), P("dp")),
        check_vma=False,
    )
```

profile of v0, /device:TPU:0, one launch (start us, length us, event | category | flops | bytes accessed | tf_op | source)
XLA Modules:
  0.0 571.0 jit_solution(17936302601688315434)
XLA Ops:
  7.2 0.0 copy-start
  7.2 0.0 all-reduce.4.cloned.1.call-start
  7.2 1.0 copy-done
  8.2 11.8 %convolution_convert_fusion.1 = bf16[256,8192]{1,0:T(8,128)(2,1)} fusion(bf16[256,1024]{1,0:T(8,128)(2,1)S(1)} %copy-done, bf16[1024,8192]{1,0:T(8,128)(2,1)} %param.14), kind=kOutput, calls=%fused_computation.9 | convolution fusion | flops 4297064448 | bytes 21495808 | tf_op jit(solution)/shard_map/dot_general | solution.py:43
  20.0 0.0 copy-start.4
  20.0 0.0 copy-start.2
  20.0 0.0 copy-start.5
  20.0 0.0 all-reduce.4.cloned.1.call-update
  20.1 0.0 all-gather.7.cloned.1.call-start
  20.1 0.7 all-gather.7.cloned.1.call-update
  20.8 0.0 all-gather.9.cloned.1.call-start
  20.9 0.7 all-gather.9.cloned.1.call-update
  21.5 0.0 all-reduce.6.cloned.1.call-start
  22.9 6.0 %all-gather.3 = f32[4,1,256]{2,1,0:T(1,128)S(1)} all-gather(f32[1,1,256]{2,1,0:T(1,128)S(1)} %fusion.13), channel_id=1, replica_groups=mesh['dp'=4,'tensor'=8] {'dp'}, dimensions={0}, use_global_device_ids=true | all-gather | bytes 5120 | tf_op jit(solution)/shard_map/all_gather | solution.py:8
  28.9 5.4 all-gather.2
  34.3 0.0 copy-done.4
  34.3 0.0 copy-done.2
  34.3 1.7 gather_fusion
  36.1 143.1 %all-reduce.4.cloned.1.call-done = bf16[256,8192]{1,0:T(8,128)(2,1)} async-done(((bf16[256,8192]{1,0:T(8,128)(2,1)}), bf16[256,8192]{1,0:T(8,128)(2,1)}) %all-reduce.4.cloned.1.call-update) | async-done | bytes 4194320 | tf_op jit(solution)/shard_map/psum | solution.py:44
  179.2 74.6 %all-gather.7.cloned.1.call-done = bf16[256,8192]{1,0:T(8,128)(2,1)} async-done(((bf16[32,8192]{1,0:T(8,128)(2,1)}), bf16[256,8192]{1,0:T(8,128)(2,1)}) %all-gather.7.cloned.1.call-update) | async-done | bytes 4194320 | tf_op jit(solution)/shard_map/all_gather | solution.py:45
  253.8 4.9 fusion
  258.7 0.0 copy-start.6
  258.7 100.9 %all-gather.9.cloned.1.call-done = bf16[8192,1024]{1,0:T(8,128)(2,1)} async-done(((bf16[2048,1024]{1,0:T(8,128)(2,1)}), bf16[8192,1024]{1,0:T(8,128)(2,1)}) %all-gather.9.cloned.1.call-update) | async-done | bytes 16777232 | tf_op jit(solution)/shard_map/all_gather | solution.py:51
  359.6 0.0 copy-done.5
  359.6 10.6 %fusion.20 = f32[256,1024]{1,0:T(8,128)S(1)} fusion(bf16[8192,1024]{1,0:T(8,128)(2,1)} %all-gather.9.cloned.1.call-done, f32[8192]{0:T(1024)S(1)} %copy-done.5, f32[256]{0:T(256)S(1)} %add_rsqrt_fusion, bf16[256,8192]{1,0:T(8,128)(2,1)} %all-reduce.4.cloned.1.call-done, bf16[256,8192]{1,0:T(8,128)(2,1)} %all-gather.7.cloned.1.call-done), kind=kOutput, calls=%fused_computation.41 | convolution fusion | flops 4311744512 | bytes 26248192 | tf_op jit(solution)/shard_map/dot_general | solution.py:49
  370.1 0.0 copy-done.6
  370.2 1.1 fusion.11
  371.2 21.4 %psum.22 = f32[256]{0:T(256)S(1)} all-reduce(f32[256]{0:T(256)S(1)} %bitcast.53), channel_id=1, replica_groups=mesh['dp'=4,'tensor'=8] {'tensor'}, use_global_device_ids=true, to_apply=%region_2.3 | all-reduce | flops 256 | bytes 2048 | tf_op jit(solution)/shard_map/psum | solution.py:56
  392.6 0.0 copy-start.3
  392.6 5.1 all-gather.1
  397.7 0.2 while.14
  397.9 2.1 scatter_custom_fusion
  400.0 0.7 convert_element_type.61
  400.7 0.0 all-reduce.6.cloned.1.call-update
  400.8 0.2 reduce-scatter.2.cloned.1.call-start
  401.0 13.8 %convolution_convert_fusion = bf16[8192,1024]{1,0:T(8,128)(2,1)} fusion(f32[256,1024]{1,0:T(8,128)S(1)} %fusion.20, f32[1024]{0:T(1024)S(1)} %copy-done.6, f32[256]{0:T(256)S(1)} %subtract_multiply_fusion, f32[8192]{0:T(1024)S(1)} %copy-done.5, f32[256]{0:T(256)S(1)} %add_rsqrt_fusion, bf16[256,8192]{1,0:T(8,128)(2,1)} %all-reduce.4.cloned.1.call-done, ...), kind=kOutput, calls=%fused_computation.6 | convolution fusion | flops 4322754560 | bytes 26253312 | tf_op jit(solution)/shard_map/dot_general | solution.py:76
  414.7 0.0 copy-done.3
  414.7 0.0 reduce-scatter.2.cloned.1.call-update
  414.8 0.6 copy-done.7
  415.4 0.6 dynamic-slice
  416.6 0.0 copy-start.1
  416.6 0.8 fusion.9
  417.4 6.7 %psum.23 = f32[1024]{0:T(1024)} all-reduce(f32[1024]{0:T(1024)S(1)} %bitcast.51), channel_id=1, replica_groups=mesh['dp'=4,'tensor'=8] {'dp'}, use_global_device_ids=true, to_apply=%region_6.7 | all-reduce | flops 1024 | bytes 8192 | tf_op jit(solution)/shard_map/psum | solution.py:64
  424.1 4.9 all-reduce.6.cloned.1.call-done
  429.1 1.6 dynamic-slice_convert_fusion
  430.7 127.1 %reduce-scatter.2.cloned.1.call-done = bf16[2048,1024]{1,0:T(8,128)(2,1)} async-done(((bf16[8192,1024]{1,0:T(8,128)(2,1)}), bf16[2048,1024]{1,0:T(8,128)(2,1)}) %reduce-scatter.2.cloned.1.call-update) | async-done | bytes 4194320 | tf_op jit(solution)/shard_map/reduce_scatter | solution.py:75
  557.8 6.6 %convert_element_type.60 = f32[2048,1024]{1,0:T(8,128)} convert(bf16[2048,1024]{1,0:T(8,128)(2,1)} %reduce-scatter.2.cloned.1.call-done) | non-fusion elementwise | flops 2097152 | bytes 12582912 | tf_op jit(solution)/shard_map/convert_element_type | solution.py:82
  564.4 0.0 copy-done.1
  (29 shorter events, 0.2 us)
Async XLA Ops:
  7.2 1.1 copy-start
  7.2 172.0 %all-reduce.4.cloned.1.call-start = ((), (), s32[]{:S(2)}) async-start(), calls=%async_computation.2 | async-start | bytes 8388608 | tf_op jit(solution)/shard_map/psum | solution.py:44
  20.0 14.3 %copy-start.4 = (s32[256]{0:T(256)S(1)}, s32[256]{0:T(256)}, u32[]{:S(2)}) copy-start(s32[256]{0:T(256)} %param.12) | copy-start | bytes 3076
  20.0 14.3 %copy-start.2 = (f32[128256]{0:T(1024)S(1)}, f32[128256]{0:T(1024)}, u32[]{:S(2)}) copy-start(f32[128256]{0:T(1024)} %param.19) | copy-start | bytes 1539076
  20.0 339.5 %copy-start.5 = (f32[8192]{0:T(1024)S(1)}, f32[8192]{0:T(1024)}, u32[]{:S(2)}) copy-start(f32[8192]{0:T(1024)} %param.16) | copy-start | bytes 98308
  20.1 233.7 %all-gather.7.cloned.1.call-start = ((), (), s32[]{:S(2)}) async-start(), calls=%async_computation.1 | async-start | bytes 4718592 | tf_op jit(solution)/shard_map/all_gather | solution.py:45
  20.8 338.7 %all-gather.9.cloned.1.call-start = ((), (), s32[]{:S(2)}) async-start(), calls=%async_computation.3 | async-start | bytes 20971520 | tf_op jit(solution)/shard_map/all_gather | solution.py:51
  21.5 407.5 %all-reduce.6.cloned.1.call-start = ((), (), s32[]{:S(2)}) async-start(), calls=%async_computation.5 | async-start | bytes 516096
  258.7 111.5 %copy-start.6 = (f32[1024]{0:T(1024)S(1)}, f32[1024]{0:T(1024)}, u32[]{:S(2)}) copy-start(f32[1024]{0:T(1024)} %param.18) | copy-start | bytes 12292
  392.6 22.1 %copy-start.3 = (f32[256]{0:T(256)}, f32[256]{0:T(256)S(1)}, u32[]{:S(2)}) copy-start(f32[256]{0:T(256)S(1)} %get-tuple-element.63) | copy-start | bytes 3076
  400.8 157.1 %reduce-scatter.2.cloned.1.call-start = ((), (), s32[]{:S(2)}) async-start(), calls=%async_computation.4 | async-start | bytes 20971520 | tf_op jit(solution)/shard_map/reduce_scatter | solution.py:75
  414.7 0.7 copy-start.7
  416.6 147.8 %copy-start.1 = (bf16[256,1024]{1,0:T(8,128)(2,1)S(1)}, bf16[256,1024]{1,0:T(8,128)(2,1)}, u32[]{:S(2)}) copy-start(bf16[256,1024]{1,0:T(8,128)(2,1)} %param.13) | copy-start | bytes 1572868
Sparse Core Ops, SparseCore 0:
  20.2 158.9 all-reduce.3
  181.3 72.3 all-gather.6
  255.3 104.1 all-gather.8
  400.9 28.1 all-reduce.5
  431.7 126.0 reduce-scatter.1
where the time goes:
time: 571 us
  waiting for transfers between devices  452 us (79%)
  blocking collectives  44.5 us (8%)
  matrix products  38 us (7%)
  other arithmetic  16.1 us (3%)
  between operations  15.9 us (3%)
    psum x1, waiting for transfers between devices, local(): lax.psum(partial_sum.astype(jnp.bfloat16), 'tensor').astype(jnp.float32)  143 us
    reduce_scatter x1, waiting for transfers between devices, local(): lax.psum_scatter(lax.dot_general(columns, d_pre, contract, preferred_elem...  127 us
    all_gather x1, waiting for transfers between devices, local(): lax.all_gather(twist_in, 'dp', axis=0, tiled=True)  101 us
    all_gather x1, waiting for transfers between devices, local(): resid_all = lax.all_gather(residual, 'tensor', axis=0, tiled=True)  74.6 us
    psum x1, blocking collectives, local(): twist_vals = lax.psum(partial_psi, 'tensor') + token_bias[token_ids]  21.4 us
    all_gather x3, blocking collectives, merged_2(): pieces = jax.tree.map(lambda part: lax.all_gather(part, axis), value)  16.4 us
    dot_general x1, matrix products, local(): lax.dot_general(columns, d_pre, contract, preferred_element_type=jnp.floa...  13.8 us
    dot_general x1, matrix products, local(): jnp.dot(attn_heads, out_proj, preferred_element_type=jnp.float32)  11.8 us
  transfers between devices with their start and end apart: 5, of which 5 were waited for; matrix products, arithmetic and copies ran while one was open for 4% of the time, Pallas kernels for 0%

commit v1 on v0

v1 whole, which is shorter than its diff:
```python
import jax
import jax.numpy as jnp
from jax import lax
from jax.sharding import PartitionSpec as P


def normalize(hidden, norm_gain):
    values = hidden.astype(jnp.float32)
    scaled = lax.rsqrt(jnp.mean(values * values, axis=-1, keepdims=True) + 1e-05)
    return (values * scaled * norm_gain[None, :]).astype(jnp.bfloat16)


def make_local(n_dp, n_tensor):
    def local(
        token_ids,
        attn_heads,
        out_proj,
        residual,
        norm_gain,
        twist_in,
        twist_out,
        token_bias,
        toxicity,
        prompt_len,
    ):
        seq_len = attn_heads.shape[0]
        rows = residual.shape[0]
        vocab_size = token_bias.shape[0]
        width = attn_heads.shape[1] * n_tensor
        feats = width // n_dp
        tokens = seq_len * n_dp
        me = lax.axis_index("dp")

        ids_all = lax.all_gather(
            jnp.concatenate([token_ids, toxicity, prompt_len]), "dp", axis=0
        )
        levels_all = ids_all[:, seq_len].astype(jnp.float32)
        prompt_all = ids_all[:, seq_len + 1]
        ids_all = ids_all[:, :seq_len]

        partial_sum = jnp.dot(attn_heads, out_proj, preferred_element_type=jnp.float32)
        summed = lax.psum_scatter(
            partial_sum.astype(jnp.bfloat16), "tensor", scatter_dimension=0, tiled=True
        ).astype(jnp.float32)
        hidden = (residual.astype(jnp.float32) + summed).astype(jnp.bfloat16)
        normed = normalize(hidden, norm_gain)
        split = lax.all_to_all(normed, "dp", split_axis=1, concat_axis=0, tiled=True)
        columns = lax.all_gather(split, "tensor", axis=0, tiled=True)
        pre_part = jnp.dot(columns, twist_in, preferred_element_type=jnp.float32)
        pre_act = lax.psum_scatter(
            pre_part.astype(jnp.bfloat16), "dp", scatter_dimension=0, tiled=True
        ).astype(jnp.float32)
        sigma = jax.nn.sigmoid(pre_act)
        active = pre_act * sigma
        slope = (twist_out[None, :] * sigma * (1.0 + pre_act * (1.0 - sigma))).astype(jnp.bfloat16)
        slope_all = lax.all_gather(slope, "dp", axis=0, tiled=True)

        span = seq_len // n_dp
        blocks = span // rows
        own_ids = lax.dynamic_slice_in_dim(ids_all, me * span, span, axis=1)
        psi = lax.psum(jnp.sum(active * twist_out[None, :], axis=1), "tensor")
        grid = psi.reshape(blocks, n_dp, rows).transpose(1, 0, 2).reshape(n_dp, span)
        grid = grid + token_bias[own_ids]
        live = (me * span + jnp.arange(span))[None, :] >= prompt_all[:, None]
        levels = levels_all[:, None] * live.astype(jnp.float32)
        highest = jnp.max(jnp.where(live, grid, -1e30), axis=0)
        expo = jnp.where(live, jnp.exp(jnp.where(live, grid - highest[None, :], -80.0)), 0.0)
        totals = jnp.sum(expo, axis=0)
        lab_sum = jnp.sum(levels, axis=0)
        weights = (
            expo / jnp.maximum(totals, 1.0)[None, :] - levels / jnp.maximum(lab_sum, 1.0)[None, :]
        ) / seq_len
        flat = weights.reshape(n_dp, blocks, rows).transpose(1, 0, 2).reshape(-1)
        grad_out_part = jnp.sum(flat[:, None] * active, axis=0)
        packed = jnp.concatenate([flat, grid.reshape(-1), grad_out_part])
        packed = lax.all_gather(packed, "dp", axis=0)
        flat_all = packed[:, :seq_len].reshape(tokens)
        grids = packed[:, seq_len : 2 * seq_len].reshape(n_dp, n_dp, span)
        twist_vals = lax.dynamic_index_in_dim(grids, me, 1, keepdims=False).reshape(seq_len)
        grad_out = jnp.sum(packed[:, 2 * seq_len :], axis=0)

        d_pre = (slope_all.astype(jnp.float32) * flat_all[:, None]).astype(jnp.bfloat16)
        contract = (((0,), (0,)), ((), ()))
        grad_in = lax.dot_general(columns, d_pre, contract, preferred_element_type=jnp.float32)

        own_vocab = vocab_size // n_dp
        ids_perm = ids_all.reshape(n_dp, n_tensor, rows).transpose(1, 0, 2).reshape(-1)
        spot = ids_perm - me * own_vocab
        spot = jnp.where((spot >= 0) & (spot < own_vocab), spot, own_vocab)
        grad_bias = jnp.zeros((own_vocab,), jnp.float32).at[spot].add(flat_all, mode="drop")
        return (twist_vals, grad_in, grad_out, grad_bias)

    return local


def solution(mesh):
    placed = (
        P("dp"),
        P("dp", "tensor"),
        P("tensor", None),
        P(("dp", "tensor"), None),
        P(),
        P("dp", "tensor"),
        P("tensor"),
        P(),
        P("dp"),
        P("dp"),
    )
    return jax.shard_map(
        make_local(mesh.shape["dp"], mesh.shape["tensor"]),
        mesh=mesh,
        in_specs=placed,
        out_specs=(P("dp"), P("dp", "tensor"), P("tensor"), P("dp")),
        check_vma=False,
    )
```

time: 571 us -> 304 us (0.53)
  waiting for transfers between devices: 452 us -> 193 us
  matrix products: 38 us -> 32 us
    psum x1 -> x0, waiting for transfers between devices: 143 us -> none  [local(): lax.psum(partial_sum.astype(jnp.bfloat16), 'tensor').astype(jnp.float32)]
    all_gather x2, waiting for transfers between devices: 175 us -> 72.3 us  [the longest x1 72.3 us: local(): columns = lax.all_gather(split, 'tensor', axis=0, tiled=True)]
    all_to_all x0 -> x1, blocking collectives: none -> 11.9 us  [local(): lax.all_to_all(normed, 'dp', split_axis=1, concat_axis=0, tiled=True)]
    all_gather x3 -> x1, blocking collectives: 16.4 us -> 5.19 us  [local(): packed = lax.all_gather(packed, 'dp', axis=0)]
    psum x2 -> x1, blocking collectives: 28 us -> 21.3 us  [local(): psi = lax.psum(jnp.sum(active * twist_out[None, :], axis=1), 'tensor')]
    unnamed x6 -> x4, waiting for transfers between devices: 6.37 us -> 0.07 us
    reduce_scatter x1 -> x2, waiting for transfers between devices: 127 us -> 121 us  [the longest x1 91.3 us: local(): lax.psum_scatter(partial_sum.astype(jnp.bfloat16), 'tensor', scatter_dime...]
    dot_general x3 -> x1, matrix products: 12.5 us -> 9.27 us  [local(): pre_part = jnp.dot(columns, twist_in, preferred_element_type=jnp.float32)]
  transfers between devices with their start and end apart: 5 -> 4, of which waited for: 5 -> 3; matrix products, arithmetic and copies ran while one was open for 4% -> 5% of each run, Pallas kernels for 0% -> 0%
where the time goes in v1:
time: 304 us
  waiting for transfers between devices  193 us (63%)
  blocking collectives  42.8 us (14%)
  matrix products  32 us (11%)
  between operations  15.9 us (5%)
  other arithmetic  14.6 us (5%)
  local copies, waits for them, and re-layouts  5.09 us (2%)
    reduce_scatter x1, waiting for transfers between devices, local(): lax.psum_scatter(partial_sum.astype(jnp.bfloat16), 'tensor', scatter_dime...  91.3 us
    all_gather x1, waiting for transfers between devices, local(): columns = lax.all_gather(split, 'tensor', axis=0, tiled=True)  72.3 us
    reduce_scatter x1, waiting for transfers between devices, local(): lax.psum_scatter(pre_part.astype(jnp.bfloat16), 'dp', scatter_dimension=0...  29.8 us
    psum x1, blocking collectives, local(): psi = lax.psum(jnp.sum(active * twist_out[None, :], axis=1), 'tensor')  21.3 us
    all_to_all x1, blocking collectives, local(): lax.all_to_all(normed, 'dp', split_axis=1, concat_axis=0, tiled=True)  11.9 us
    dot_general x1, matrix products, local(): jnp.dot(attn_heads, out_proj, preferred_element_type=jnp.float32)  11.8 us
    dot_general x1, matrix products, local(): lax.dot_general(columns, d_pre, contract, preferred_element_type=jnp.floa...  10.9 us
    dot_general x1, matrix products, local(): pre_part = jnp.dot(columns, twist_in, preferred_element_type=jnp.float32)  9.27 us
  transfers between devices with their start and end apart: 4, of which 3 were waited for; matrix products, arithmetic and copies ran while one was open for 5% of the time, Pallas kernels for 0%

profile of v1, /device:TPU:0, one launch (start us, length us, event | category | flops | bytes accessed | tf_op | source)
XLA Modules:
  0.0 304.0 jit_solution(6250927243284886044)
XLA Ops:
  7.2 0.0 copy-start
  7.2 0.0 reduce-scatter.3.cloned.1.call-start
  7.2 1.0 copy-done
  8.2 11.8 %convolution_convert_fusion = bf16[256,8192]{1,0:T(8,128)(2,1)} fusion(bf16[256,1024]{1,0:T(8,128)(2,1)S(1)} %copy-done, bf16[1024,8192]{1,0:T(8,128)(2,1)} %param.12), kind=kOutput, calls=%fused_computation.3 | convolution fusion | flops 4297064448 | bytes 21495808 | tf_op jit(solution)/shard_map/dot_general | solution.py:41
  20.0 0.0 reduce-scatter.3.cloned.1.call-update
  20.1 0.0 all-gather.6.cloned.1.call-start
  20.1 91.3 %reduce-scatter.3.cloned.1.call-done = bf16[32,8192]{1,0:T(8,128)(2,1)} async-done(((bf16[256,8192]{1,0:T(8,128)(2,1)}), bf16[32,8192]{1,0:T(8,128)(2,1)}) %reduce-scatter.3.cloned.1.call-update) | async-done | bytes 524304 | tf_op jit(solution)/shard_map/reduce_scatter | solution.py:42
  111.4 1.3 fusion.7
  112.7 1.2 fusion.9
  114.0 11.9 %all_to_all.19 = bf16[32,4,2048]{2,0,1:T(8,128)(2,1)} all-to-all(bf16[32,4,2048]{2,0,1:T(8,128)(2,1)S(1)} %bitcast.28), channel_id=1, replica_groups=mesh['dp'=4,'tensor'=8] {'dp'}, dimensions={1} | all-to-all | bytes 1048576 | tf_op jit(solution)/shard_map/all_to_all | solution.py:47
  125.9 0.0 all-gather.6.cloned.1.call-update
  126.0 0.0 copy-start.4
  126.0 0.0 copy-start.6
  126.0 0.0 reduce-scatter.5.cloned.1.call-start
  126.1 72.3 %all-gather.6.cloned.1.call-done = bf16[1024,2048]{1,0:T(8,128)(2,1)} async-done(((bf16[128,2048]{1,0:T(8,128)(2,1)}), bf16[1024,2048]{1,0:T(8,128)(2,1)}) %all-gather.6.cloned.1.call-update) | async-done | bytes 4194320 | tf_op jit(solution)/shard_map/all_gather | solution.py:48
  198.4 9.3 %convolution_convert_fusion.1 = bf16[1024,1024]{1,0:T(8,128)(2,1)} fusion(bf16[1024,2048]{1,0:T(8,128)(2,1)} %all-gather.6.cloned.1.call-done, bf16[2048,1024]{1,0:T(8,128)(2,1)} %param.15), kind=kOutput, calls=%fused_computation.7 | convolution fusion | flops 4296015872 | bytes 10485760 | tf_op jit(solution)/shard_map/dot_general | solution.py:49
  207.7 0.0 reduce-scatter.5.cloned.1.call-update
  207.7 0.0 all-gather.8.cloned.1.call-start
  207.7 29.8 %reduce-scatter.5.cloned.1.call-done = bf16[256,1024]{1,0:T(8,128)(2,1)} async-done(((bf16[1024,1024]{1,0:T(8,128)(2,1)}), bf16[256,1024]{1,0:T(8,128)(2,1)}) %reduce-scatter.5.cloned.1.call-update) | async-done | bytes 524304 | tf_op jit(solution)/shard_map/reduce_scatter | solution.py:50
  237.5 2.4 fusion.15
  239.9 0.0 all-gather.8.cloned.1.call-update
  241.2 0.6 dynamic-slice
  242.5 0.2 add_dynamic-update-slice_fusion
  242.7 4.3 %all-reduce = s32[1032]{0:T(1024)S(1)} all-reduce(s32[1032]{0:T(1024)S(1)} %add_dynamic-update-slice_fusion), channel_id=2, replica_groups=mesh['dp'=4,'tensor'=8] {'dp'}, use_global_device_ids=true, to_apply=%add | all-reduce | flops 1032 | bytes 8256
  247.0 0.1 reshape.180
  247.1 0.1 compare_select_fusion.1
  247.2 0.1 reshape.166
  247.2 1.7 gather_fusion
  249.0 0.1 gather.8
  249.1 0.2 slice_reduce_fusion.1
  249.2 0.1 fusion.22
  249.4 0.1 select_reduce_fusion.1
  249.5 0.1 max.19
  249.5 0.1 sub.45
  249.6 0.1 sub.47
  249.7 0.1 reshape.159
  249.8 21.3 %psum.7 = f32[4,2,32]{2,0,1:T(4,128)S(1)} all-reduce(f32[4,2,32]{2,0,1:T(4,128)S(1)} %bitcast.32), channel_id=1, replica_groups=mesh['dp'=4,'tensor'=8] {'tensor'}, use_global_device_ids=true, to_apply=%region_4.0 | all-reduce | flops 256 | bytes 2048 | tf_op jit(solution)/shard_map/psum | solution.py:61
  271.2 0.1 fusion.27
  271.3 0.1 fusion.21
  271.4 0.1 reshape.160
  271.5 0.1 reshape.161
  271.5 1.4 multiply_reduce_fusion
  273.0 5.2 %all-gather.2 = f32[4,1,1536]{2,1,0:T(1,128)S(1)} all-gather(f32[1,1,1536]{2,1,0:T(1,128)S(1)} %reshape.189), channel_id=3, replica_groups=mesh['dp'=4,'tensor'=8] {'dp'}, dimensions={0}, use_global_device_ids=true | all-gather | bytes 30720 | tf_op jit(solution)/shard_map/all_gather | solution.py:76
  278.2 0.1 reshape.162
  278.3 0.6 reshape.163
  278.9 7.0 %scatter_custom_fusion = f32[32064]{0:T(1024)} fusion(s32[1024]{0:T(1024)S(1)} %bitcast.33, f32[1024]{0:T(1024)S(1)} %bitcast.34, f32[]{:T(128)} %constant.19.clone.1), kind=kCustom, calls=%fused_computation.30 | custom fusion | flops 1024 | bytes 128260 | tf_op jit(solution)/shard_map/scatter-add | solution.py:90
  285.9 0.6 slice_reduce_fusion
  286.5 10.9 %fusion.1 = f32[2048,1024]{1,0:T(8,128)} fusion(bf16[1024,2048]{1,0:T(8,128)(2,1)} %all-gather.6.cloned.1.call-done, bf16[1024,1024]{1,0:T(8,128)(2,1)} %all-gather.8.cloned.1.call-done, f32[1024]{0:T(1024)S(1)} %bitcast.35), kind=kOutput, calls=%fused_computation.5 | convolution fusion | flops 4298113024 | bytes 14684160 | tf_op jit(solution)/shard_map/dot_general | solution.py:84
  (30 shorter events, 0.2 us)
Async XLA Ops:
  7.2 1.0 copy-start
  7.2 104.2 %reduce-scatter.3.cloned.1.call-start = ((), (), s32[]{:S(2)}) async-start(), calls=%async_computation.3 | async-start | bytes 4718592 | tf_op jit(solution)/shard_map/reduce_scatter | solution.py:42
  20.0 91.4 %copy-start.2 = (bf16[32,8192]{1,0:T(8,128)(2,1)S(1)}, bf16[32,8192]{1,0:T(8,128)(2,1)}, u32[]{:S(2)}) copy-start(bf16[32,8192]{1,0:T(8,128)(2,1)} %param.13) | copy-start | bytes 1572868
  20.0 92.7 %copy-start.3 = (f32[8192]{0:T(1024)S(1)}, f32[8192]{0:T(1024)}, u32[]{:S(2)}) copy-start(f32[8192]{0:T(1024)} %param.14) | copy-start | bytes 98308
  20.1 178.3 %all-gather.6.cloned.1.call-start = ((), (), s32[]{:S(2)}) async-start(), calls=%async_computation.4 | async-start | bytes 4718592 | tf_op jit(solution)/shard_map/all_gather | solution.py:48
  126.0 111.6 %copy-start.4 = (f32[1024]{0:T(1024)S(1)}, f32[1024]{0:T(1024)}, u32[]{:S(2)}) copy-start(f32[1024]{0:T(1024)} %param.16) | copy-start | bytes 12292
  126.0 115.2 %copy-start.6 = (u32[32]{0:T(128)S(1)}, u32[32]{0:T(128)}, u32[]{:S(2)}) copy-start(u32[32]{0:T(128)} %constant.50) | copy-start | bytes 388
  126.0 116.5 %copy-start.5 = (s32[256]{0:T(256)S(1)}, s32[256]{0:T(256)}, u32[]{:S(2)}) copy-start(s32[256]{0:T(256)} %param.10) | copy-start | bytes 3076
  126.0 111.5 %reduce-scatter.5.cloned.1.call-start = ((), (), s32[]{:S(2)}) async-start(), calls=%async_computation.5 | async-start | bytes 2621440 | tf_op jit(solution)/shard_map/reduce_scatter | solution.py:50
  207.7 39.6 %copy-start.1 = (f32[128256]{0:T(1024)S(1)}, f32[128256]{0:T(1024)}, u32[]{:S(2)}) copy-start(f32[128256]{0:T(1024)} %param.17) | copy-start | bytes 1539076
  207.7 78.9 %all-gather.8.cloned.1.call-start = ((), (), s32[]{:S(2)}) async-start(), calls=%async_computation.6 | async-start | bytes 2621440 | tf_op jit(solution)/shard_map/all_gather | solution.py:56
Sparse Core Ops, SparseCore 0:
  20.2 91.1 reduce-scatter.2
  126.1 72.2 all-gather.5
  207.8 29.6 reduce-scatter.4
  240.0 22.5 all-gather.7

commit v2 on v1

--- a/solution.py
+++ b/solution.py
@@ -1,13 +1,248 @@
+import functools
+
 import jax
 import jax.numpy as jnp
 from jax import lax
+from jax.experimental import pallas as pl
+from jax.experimental.pallas import tpu as pltpu
 from jax.sharding import PartitionSpec as P
 
-
-def normalize(hidden, norm_gain):
-    values = hidden.astype(jnp.float32)
-    scaled = lax.rsqrt(jnp.mean(values * values, axis=-1, keepdims=True) + 1e-05)
-    return (values * scaled * norm_gain[None, :]).astype(jnp.bfloat16)
+PIECES = 2
+MESH = pl.DeviceIdType.MESH
+
+
+def ring_kernel(
+    n_dp,
+    n,
+    part_ref,
+    resid_ref,
+    gain_ref,
+    twist_ref,
+    pre_ref,
+    cols_ref,
+    slots,
+    hid,
+    normed,
+    outbox,
+    inbox,
+    sum_send,
+    sum_recv,
+    swap_send,
+    swap_recv,
+    ring_send,
+    ring_recv,
+    pre_send,
+    pre_recv,
+):
+    rows, width = resid_ref.shape
+    feats = width // n_dp
+    half = n_dp // 2
+    per = n // n_dp
+    piece = width // (2 * PIECES)
+    me = lax.axis_index("dp")
+    t_me = lax.axis_index("tensor")
+
+    def spot_of(t):
+        return jnp.where(t % 2 == 0, t // 2, n - 1 - t // 2)
+
+    def index_of(p):
+        p = lax.rem(p + 2 * n, n)
+        return jnp.where(p < n // 2, 2 * p, 2 * (n - 1 - p) + 1)
+
+    p = spot_of(t_me)
+    near = (index_of(p + 1), index_of(p - 1))
+    back = (-1, 1)
+
+    barrier = pltpu.get_barrier_semaphore()
+    for t in near:
+        pl.semaphore_signal(barrier, inc=1, device_id=(me, t), device_id_type=MESH)
+    for step in range(1, n_dp):
+        peer = lax.rem(me + step, n_dp)
+        pl.semaphore_signal(barrier, inc=1, device_id=(peer, t_me), device_id_type=MESH)
+    pl.semaphore_wait(barrier, n_dp + 1)
+
+    def span(way, q):
+        return pl.ds((way * PIECES + q) * piece, piece)
+
+    def sum_copy(way, q, step, first):
+        if first:
+            source = part_ref.at[index_of(p + back[way]), :, span(way, q)]
+        else:
+            source = slots.at[way, q, step - 1]
+        return pltpu.make_async_remote_copy(
+            src_ref=source,
+            dst_ref=slots.at[way, q, step],
+            send_sem=sum_send.at[way, q, step],
+            recv_sem=sum_recv.at[way, q, step],
+            device_id=(me, near[way]),
+            device_id_type=MESH,
+        )
+
+    for q in range(PIECES):
+        for way in range(2):
+            sum_copy(way, q, 0, True).start()
+
+    def sum_step(step, carry):
+        for q in range(PIECES):
+            for way in range(2):
+                sum_copy(way, q, step - 1, True).wait_recv()
+                t = index_of(p + back[way] * (step + 1))
+                mine = part_ref[t, :, span(way, q)].astype(jnp.float32)
+                so_far = slots[way, q, step - 1].astype(jnp.float32)
+                slots[way, q, step - 1] = (so_far + mine).astype(jnp.bfloat16)
+                sum_copy(way, q, step, False).start()
+        return carry
+
+    lax.fori_loop(1, n - 1, sum_step, 0)
+    for q in range(PIECES):
+        for way in range(2):
+            sum_copy(way, q, n - 2, True).wait_recv()
+            mine = part_ref[t_me, :, span(way, q)].astype(jnp.float32)
+            so_far = slots[way, q, n - 2].astype(jnp.float32)
+            total = resid_ref[:, span(way, q)].astype(jnp.float32) + (so_far + mine)
+            hid[:, span(way, q)] = total.astype(jnp.bfloat16)
+
+    squares = jnp.zeros((rows, 1), jnp.float32)
+    for i in range(n_dp):
+        values = hid[:, pl.ds(i * feats, feats)].astype(jnp.float32)
+        squares = squares + jnp.sum(values * values, axis=1, keepdims=True)
+    scaled = lax.rsqrt(squares / width + 1e-05)
+    for i in range(n_dp):
+        values = hid[:, pl.ds(i * feats, feats)].astype(jnp.float32)
+        gains = gain_ref[:, pl.ds(i * feats, feats)]
+        normed[i] = (values * scaled * gains).astype(jnp.bfloat16)
+
+    def swap_copy(peer, source):
+        return pltpu.make_async_remote_copy(
+            src_ref=normed.at[peer],
+            dst_ref=cols_ref.at[t_me, source],
+            send_sem=swap_send.at[peer],
+            recv_sem=swap_recv.at[source],
+            device_id=(peer, t_me),
+            device_id_type=MESH,
+        )
+
+    for step in range(1, n_dp):
+        peer = lax.rem(me + step, n_dp)
+        swap_copy(peer, me).start()
+    cols_ref[t_me, me] = normed[me]
+    for step in range(1, n_dp):
+        peer = lax.rem(me + step, n_dp)
+        swap_copy(peer, peer).wait_recv()
+
+    def ring_copy(way, step):
+        t = index_of(p + back[way] * step)
+        place = cols_ref.at[t, pl.ds(way * half, half)]
+        return pltpu.make_async_remote_copy(
+            src_ref=place,
+            dst_ref=place,
+            send_sem=ring_send.at[way, step],
+            recv_sem=ring_recv.at[way, step],
+            device_id=(me, near[way]),
+            device_id_type=MESH,
+        )
+
+    def pre_copy(t, way, source):
+        owner = t // per
+        local = lax.rem(t, per)
+        return pltpu.make_async_remote_copy(
+            src_ref=outbox.at[t, way],
+            dst_ref=inbox.at[source, local, way],
+            send_sem=pre_send.at[t, way],
+            recv_sem=pre_recv.at[source, local, way],
+            device_id=(owner, t_me),
+            device_id_type=MESH,
+        )
+
+    def multiply(t, way):
+        block = cols_ref[t, pl.ds(way * half, half)].reshape(half * rows, feats)
+        found = jnp.dot(block, twist_ref[...], preferred_element_type=jnp.float32)
+        outbox[t, way] = found.astype(jnp.bfloat16)
+        owner = t // per
+
+        @pl.when(owner != me)
+        def _():
+            pre_copy(t, way, me).start()
+
+    def ring_step(step, carry):
+        for way in range(2):
+
+            @pl.when(step > 0)
+            def _():
+                before = ring_copy(way, step - 1)
+                before.wait_recv()
+
+            @pl.when(step < n - 1)
+            def _():
+                ring_copy(way, step).start()
+
+        for way in range(2):
+            multiply(index_of(p + back[way] * step), way)
+        return carry
+
+    lax.fori_loop(0, n, ring_step, 0)
+
+    for local in range(per):
+        for way in range(2):
+            total = outbox[me * per + local, way].astype(jnp.float32)
+            for step in range(1, n_dp):
+                peer = lax.rem(me + step, n_dp)
+                pre_copy(me * per + local, way, peer).wait_recv()
+                total = total + inbox[peer, local, way].astype(jnp.float32)
+            pre_ref[local, way] = total
+
+    for step in range(1, n_dp):
+        peer = lax.rem(me + step, n_dp)
+        swap_copy(peer, me).wait_send()
+        for local in range(per):
+            for way in range(2):
+                pre_copy(peer * per + local, way, me).wait_send()
+
+    def finish(step, carry):
+        for way in range(2):
+            for q in range(PIECES):
+                sum_copy(way, q, step, True).wait_send()
+            ring_copy(way, step).wait_send()
+        return carry
+
+    lax.fori_loop(0, n - 1, finish, 0)
+
+
+def ring_call(n_dp, n, part, resid, gain, twist):
+    rows, width = resid.shape
+    feats, units = twist.shape
+    half, per = n_dp // 2, n // n_dp
+    piece = width // (2 * PIECES)
+    dma = pltpu.SemaphoreType.DMA
+    vmem = pl.BlockSpec(memory_space=pltpu.VMEM)
+    pre_act, columns = pl.pallas_call(
+        functools.partial(ring_kernel, n_dp, n),
+        out_shape=(
+            jax.ShapeDtypeStruct((per, 2, half * rows, units), jnp.float32),
+            jax.ShapeDtypeStruct((n, n_dp, rows, feats), jnp.bfloat16),
+        ),
+        in_specs=[vmem] * 4,
+        out_specs=(vmem, vmem),
+        scratch_shapes=[
+            pltpu.VMEM((2, PIECES, n - 1, rows, piece), jnp.bfloat16),
+            pltpu.VMEM((rows, width), jnp.bfloat16),
+            pltpu.VMEM((n_dp, rows, feats), jnp.bfloat16),
+            pltpu.VMEM((n, 2, half * rows, units), jnp.bfloat16),
+            pltpu.VMEM((n_dp, per, 2, half * rows, units), jnp.bfloat16),
+            dma((2, PIECES, n - 1)),
+            dma((2, PIECES, n - 1)),
+            dma((n_dp,)),
+            dma((n_dp,)),
+            dma((2, n - 1)),
+            dma((2, n - 1)),
+            dma((n, 2)),
+            dma((n_dp, per, 2)),
+        ],
+        compiler_params=pltpu.CompilerParams(
+            collective_id=0, has_side_effects=True, vmem_limit_bytes=44 * 1024 * 1024
+        ),
+    )(part.reshape(n, rows, width), resid, gain.reshape(1, width), twist)
+    return pre_act.reshape(per * n_dp * rows, units), columns.reshape(n * n_dp * rows, feats)
 
 
 def make_local(n_dp, n_tensor):
@@ -26,8 +261,6 @@
         seq_len = attn_heads.shape[0]
         rows = residual.shape[0]
         vocab_size = token_bias.shape[0]
-        width = attn_heads.shape[1] * n_tensor
-        feats = width // n_dp
         tokens = seq_len * n_dp
         me = lax.axis_index("dp")
 
@@ -39,17 +272,9 @@
         ids_all = ids_all[:, :seq_len]
 
         partial_sum = jnp.dot(attn_heads, out_proj, preferred_element_type=jnp.float32)
-        summed = lax.psum_scatter(
-            partial_sum.astype(jnp.bfloat16), "tensor", scatter_dimension=0, tiled=True
-        ).astype(jnp.float32)
-        hidden = (residual.astype(jnp.float32) + summed).astype(jnp.bfloat16)
-        normed = normalize(hidden, norm_gain)
-        split = lax.all_to_all(normed, "dp", split_axis=1, concat_axis=0, tiled=True)
-        columns = lax.all_gather(split, "tensor", axis=0, tiled=True)
-        pre_part = jnp.dot(columns, twist_in, preferred_element_type=jnp.float32)
-        pre_act = lax.psum_scatter(
-            pre_part.astype(jnp.bfloat16), "dp", scatter_dimension=0, tiled=True
-        ).astype(jnp.float32)
+        pre_act, columns = ring_call(
+            n_dp, n_tensor, partial_sum.astype(jnp.bfloat16), residual, norm_gain, twist_in
+        )
         sigma = jax.nn.sigmoid(pre_act)
         active = pre_act * sigma
         slope = (twist_out[None, :] * sigma * (1.0 + pre_act * (1.0 - sigma))).astype(jnp.bfloat16)

time: 304 us -> 193 us (0.63)
  waiting for transfers between devices: 193 us -> 0.02 us
  Pallas kernels: 0 us -> 111 us
  blocking collectives: 42.8 us -> 27.8 us
  matrix products: 32 us -> 21.4 us
  other arithmetic: 14.6 us -> 9.88 us
    reduce_scatter x2 -> x0, waiting for transfers between devices: 121 us -> none  [the longest x1 91.3 us: local(): lax.psum_scatter(partial_sum.astype(jnp.bfloat16), 'tensor', scatter_dime...]
    pallas_call x0 -> x1, Pallas kernels: none -> 111 us  [ring_call(): pl.pallas_call(functools.partial(ring_kernel, n_dp, n), out_shape=(jax.Sh...]
    all_gather x1 -> x0, waiting for transfers between devices: 72.3 us -> none  [local(): columns = lax.all_gather(split, 'tensor', axis=0, tiled=True)]
    all_to_all x1 -> x0, blocking collectives: 11.9 us -> none  [local(): lax.all_to_all(normed, 'dp', split_axis=1, concat_axis=0, tiled=True)]
    dot_general x1 -> x0, matrix products: 9.27 us -> none  [local(): pre_part = jnp.dot(columns, twist_in, preferred_element_type=jnp.float32)]
    psum x1, blocking collectives: 21.3 us -> 18.3 us  [local(): psi = lax.psum(jnp.sum(active * twist_out[None, :], axis=1), 'tensor')]
  transfers between devices with their start and end apart: 4 -> 1, of which waited for: 3 -> 0; matrix products, arithmetic and copies ran while one was open for 5% -> 7% of each run, Pallas kernels for 0% -> 0%
where the time goes in v2:
time: 193 us
  Pallas kernels  111 us (58%)
  blocking collectives  27.8 us (14%)
  matrix products  21.4 us (11%)
  between operations  16.2 us (8%)
  other arithmetic  9.88 us (5%)
  local copies, waits for them, and re-layouts  7.04 us (4%)
    pallas_call x1, Pallas kernels, ring_call(): pl.pallas_call(functools.partial(ring_kernel, n_dp, n), out_shape=(jax.Sh...  111 us
    psum x1, blocking collectives, local(): psi = lax.psum(jnp.sum(active * twist_out[None, :], axis=1), 'tensor')  18.3 us
    dot_general x1, matrix products, local(): lax.dot_general(columns, d_pre, contract, preferred_element_type=jnp.floa...  10.9 us
    dot_general x1, matrix products, local(): jnp.dot(attn_heads, out_proj, preferred_element_type=jnp.float32)  10.5 us
    scatter-add x1, other arithmetic, local(): jnp.zeros((own_vocab,), jnp.float32).at[spot].add(flat_all, mode='drop')  6.71 us
    all_gather x1, blocking collectives, local(): packed = lax.all_gather(packed, 'dp', axis=0)  5.19 us
    unnamed x1, blocking collectives  4.31 us
  transfers between devices with their start and end apart: 1, of which 0 were waited for; matrix products, arithmetic and copies ran while one was open for 7% of the time, Pallas kernels for 0%

profile of v2, /device:TPU:0, one launch (start us, length us, event | category | flops | bytes accessed | tf_op | source)
XLA Modules:
  0.0 193.0 jit_solution(14718521228968744566)
XLA Ops:
  7.2 0.0 copy-start
  7.2 0.0 copy-start.1
  7.2 0.0 copy-start.2
  7.2 0.0 all-gather.5.cloned.1.call-start
  7.2 1.0 copy-done
  8.2 10.5 %convolution_convert_fusion = bf16[256,8192]{1,0:T(8,128)(2,1)S(1)} fusion(bf16[256,1024]{1,0:T(8,128)(2,1)S(1)} %copy-done, bf16[1024,8192]{1,0:T(8,128)(2,1)} %param.12), kind=kOutput, calls=%fused_computation.3 | convolution fusion | flops 4297064448 | bytes 21495808 | tf_op jit(solution)/shard_map/dot_general | solution.py:274
  18.7 0.0 copy-done.1
  18.7 0.0 copy-done.2
  18.7 0.0 copy-start.5
  18.8 0.0 copy-start.7
  18.8 0.0 copy-start.6
  18.8 0.0 copy-start.4
  18.8 110.6 %shard_map.129 = (f32[2,2,64,1024]{3,2,1,0:T(8,128)S(1)}, bf16[8,4,32,2048]{3,2,1,0:T(8,128)(2,1)S(1)}) custom-call(bf16[8,32,8192]{2,1,0:T(8,128)(2,1)S(1)} %bitcast.37, bf16[32,8192]{1,0:T(8,128)(2,1)S(1)} %copy-done.1, f32[1,8192]{1,0:T(1,128)S(1)} %bitcast.38, bf16[2048,1024]{1,0:T(8,128)(2,1)} %twist_ref.1), custom_call_target="tpu_custom_call" | custom-call | tf_op jit(solution)/shard_map/pallas_call | solution.py:218
  129.4 0.0 copy-start.3
  129.4 1.9 copy-done.3
  131.3 0.0 copy-done.5
  131.3 1.2 fusion.12
  132.5 0.0 all-gather.5.cloned.1.call-update
  133.8 0.0 copy-done.7
  133.8 0.6 dynamic-slice
  135.1 0.2 add_dynamic-update-slice_fusion
  135.3 4.3 %all-reduce = s32[1032]{0:T(1024)S(1)} all-reduce(s32[1032]{0:T(1024)S(1)} %add_dynamic-update-slice_fusion), channel_id=2, replica_groups=mesh['dp'=4,'tensor'=8] {'dp'}, use_global_device_ids=true, to_apply=%add | all-reduce | flops 1032 | bytes 8256
  139.6 0.1 reshape.196
  139.7 0.4 multiply_reduce_fusion.1
  140.1 0.1 reshape.172
  140.2 0.1 compare_select_fusion.1
  140.2 0.1 reshape.182
  140.3 1.7 gather_fusion
  142.1 0.1 gather.8
  142.1 0.2 slice_reduce_fusion.1
  142.3 0.1 fusion.19
  142.4 0.1 select_reduce_fusion.1
  142.5 0.1 max.19
  142.6 18.3 %psum.7 = f32[4,2,32]{2,0,1:T(4,128)S(1)} all-reduce(f32[4,2,32]{2,0,1:T(4,128)S(1)} %bitcast.43), channel_id=1, replica_groups=mesh['dp'=4,'tensor'=8] {'tensor'}, use_global_device_ids=true, to_apply=%region_1.0 | all-reduce | flops 256 | bytes 2048 | tf_op jit(solution)/shard_map/psum | solution.py:286
  160.9 0.1 fusion.24
  161.1 0.1 fusion.18
  161.1 0.1 mul.79
  161.2 0.1 reshape.173
  161.3 0.1 reshape.174
  161.4 0.3 multiply_reduce_fusion
  161.7 5.2 %all-gather.2 = f32[4,1,1536]{2,1,0:T(1,128)S(1)} all-gather(f32[1,1,1536]{2,1,0:T(1,128)S(1)} %reshape.205), channel_id=3, replica_groups=mesh['dp'=4,'tensor'=8] {'dp'}, dimensions={0}, use_global_device_ids=true | all-gather | bytes 30720 | tf_op jit(solution)/shard_map/all_gather | solution.py:301
  166.9 0.1 reshape.175
  167.0 0.6 reshape.176
  167.7 0.1 sub.45
  167.8 0.1 sub.47
  167.9 6.7 %scatter_custom_fusion = f32[32064]{0:T(1024)} fusion(s32[1024]{0:T(1024)S(1)} %bitcast.46, f32[1024]{0:T(1024)S(1)} %bitcast.44, f32[]{:T(128)} %constant.18.clone.1), kind=kCustom, calls=%fused_computation.22 | custom fusion | flops 1024 | bytes 128260 | tf_op jit(solution)/shard_map/scatter-add | solution.py:315
  174.6 0.6 slice_reduce_fusion
  175.2 10.9 %fusion.1 = f32[2048,1024]{1,0:T(8,128)} fusion(bf16[1024,2048]{1,0:T(8,128)(2,1)} %bitcast.39, bf16[1024,1024]{1,0:T(8,128)(2,1)} %all-gather.5.cloned.1.call-done, f32[1024]{0:T(1024)S(1)} %bitcast.45), kind=kOutput, calls=%fused_computation.5 | convolution fusion | flops 4298113024 | bytes 14684160 | tf_op jit(solution)/shard_map/dot_general | solution.py:309
  (20 shorter events, 0.1 us)
Async XLA Ops:
  7.2 1.0 copy-start
  7.2 11.5 %copy-start.1 = (bf16[32,8192]{1,0:T(8,128)(2,1)S(1)}, bf16[32,8192]{1,0:T(8,128)(2,1)}, u32[]{:S(2)}) copy-start(bf16[32,8192]{1,0:T(8,128)(2,1)} %resid_ref.1) | copy-start | bytes 1572868
  7.2 11.5 %copy-start.2 = (f32[8192]{0:T(1024)S(1)}, f32[8192]{0:T(1024)}, u32[]{:S(2)}) copy-start(f32[8192]{0:T(1024)} %param.14) | copy-start | bytes 98308
  7.2 168.0 %all-gather.5.cloned.1.call-start = ((), (), s32[]{:S(2)}) async-start(), calls=%async_computation | async-start | bytes 2621440 | tf_op jit(solution)/shard_map/all_gather | solution.py:281
  18.7 112.6 %copy-start.5 = (f32[1024]{0:T(1024)S(1)}, f32[1024]{0:T(1024)}, u32[]{:S(2)}) copy-start(f32[1024]{0:T(1024)} %param.16) | copy-start | bytes 12292
  18.8 115.1 %copy-start.7 = (u32[32]{0:T(128)S(1)}, u32[32]{0:T(128)}, u32[]{:S(2)}) copy-start(u32[32]{0:T(128)} %constant.45) | copy-start | bytes 388
  18.8 116.3 %copy-start.6 = (s32[256]{0:T(256)S(1)}, s32[256]{0:T(256)}, u32[]{:S(2)}) copy-start(s32[256]{0:T(256)} %param.10) | copy-start | bytes 3076
  18.8 121.5 %copy-start.4 = (f32[128256]{0:T(1024)S(1)}, f32[128256]{0:T(1024)}, u32[]{:S(2)}) copy-start(f32[128256]{0:T(1024)} %param.17) | copy-start | bytes 1539076
  129.4 1.9 copy-start.3
Sparse Core Ops, SparseCore 0:
  132.7 20.3 all-gather.4

commit v3 on v2

--- a/solution.py
+++ b/solution.py
@@ -18,13 +18,19 @@
     resid_ref,
     gain_ref,
     twist_ref,
-    pre_ref,
+    head_ref,
+    meta_ref,
+    act_ref,
     cols_ref,
+    slope_ref,
+    psi_ref,
+    metas_ref,
     slots,
     hid,
     normed,
     outbox,
     inbox,
+    psi_box,
     sum_send,
     sum_recv,
     swap_send,
@@ -33,12 +39,19 @@
     ring_recv,
     pre_send,
     pre_recv,
+    meta_send,
+    meta_recv,
+    slope_send,
+    slope_recv,
+    psi_send,
+    psi_recv,
 ):
     rows, width = resid_ref.shape
     feats = width // n_dp
     half = n_dp // 2
     per = n // n_dp
     piece = width // (2 * PIECES)
+    block = half * rows
     me = lax.axis_index("dp")
     t_me = lax.axis_index("tensor")
 
@@ -54,12 +67,13 @@
     back = (-1, 1)
 
     barrier = pltpu.get_barrier_semaphore()
-    for t in near:
+    for step in range(1, n):
+        t = lax.rem(t_me + step, n)
         pl.semaphore_signal(barrier, inc=1, device_id=(me, t), device_id_type=MESH)
     for step in range(1, n_dp):
         peer = lax.rem(me + step, n_dp)
         pl.semaphore_signal(barrier, inc=1, device_id=(peer, t_me), device_id_type=MESH)
-    pl.semaphore_wait(barrier, n_dp + 1)
+    pl.semaphore_wait(barrier, n_dp + n - 2)
 
     def span(way, q):
         return pl.ds((way * PIECES + q) * piece, piece)
@@ -81,6 +95,20 @@
     for q in range(PIECES):
         for way in range(2):
             sum_copy(way, q, 0, True).start()
+
+    def meta_copy(peer, source):
+        return pltpu.make_async_remote_copy(
+            src_ref=meta_ref,
+            dst_ref=metas_ref.at[source],
+            send_sem=meta_send.at[peer],
+            recv_sem=meta_recv.at[source],
+            device_id=(peer, t_me),
+            device_id_type=MESH,
+        )
+
+    for step in range(1, n_dp):
+        meta_copy(lax.rem(me + step, n_dp), me).start()
+    metas_ref[me] = meta_ref[...]
 
     def sum_step(step, carry):
         for q in range(PIECES):
@@ -130,14 +158,14 @@
         peer = lax.rem(me + step, n_dp)
         swap_copy(peer, peer).wait_recv()
 
-    def ring_copy(way, step):
+    def ring_copy(way, step, i):
         t = index_of(p + back[way] * step)
-        place = cols_ref.at[t, pl.ds(way * half, half)]
+        place = cols_ref.at[t, way * half + i]
         return pltpu.make_async_remote_copy(
             src_ref=place,
             dst_ref=place,
-            send_sem=ring_send.at[way, step],
-            recv_sem=ring_recv.at[way, step],
+            send_sem=ring_send.at[way, step, i],
+            recv_sem=ring_recv.at[way, step, i],
             device_id=(me, near[way]),
             device_id_type=MESH,
         )
@@ -155,8 +183,8 @@
         )
 
     def multiply(t, way):
-        block = cols_ref[t, pl.ds(way * half, half)].reshape(half * rows, feats)
-        found = jnp.dot(block, twist_ref[...], preferred_element_type=jnp.float32)
+        found = cols_ref[t, pl.ds(way * half, half)].reshape(block, feats)
+        found = jnp.dot(found, twist_ref[...], preferred_element_type=jnp.float32)
         outbox[t, way] = found.astype(jnp.bfloat16)
         owner = t // per
 
@@ -165,16 +193,16 @@
             pre_copy(t, way, me).start()
 
     def ring_step(step, carry):
-        for way in range(2):
-
-            @pl.when(step > 0)
-            def _():
-                before = ring_copy(way, step - 1)
-                before.wait_recv()
-
-            @pl.when(step < n - 1)
-            def _():
-                ring_copy(way, step).start()
+        for i in range(half):
+            for way in range(2):
+
+                @pl.when(step > 0)
+                def _():
+                    ring_copy(way, step - 1, i).wait_recv()
+
+                @pl.when(step < n - 1)
+                def _():
+                    ring_copy(way, step, i).start()
 
         for way in range(2):
             multiply(index_of(p + back[way] * step), way)
@@ -189,7 +217,75 @@
                 peer = lax.rem(me + step, n_dp)
                 pre_copy(me * per + local, way, peer).wait_recv()
                 total = total + inbox[peer, local, way].astype(jnp.float32)
-            pre_ref[local, way] = total
+            sigma = 1.0 / (1.0 + jnp.exp(-total))
+            act_ref[pl.ds((local * 2 + way) * block, block)] = total * sigma
+            slope = head_ref[0:1, :] * sigma * (1.0 + total * (1.0 - sigma))
+            slope_ref[me, local, way] = slope.astype(jnp.bfloat16)
+
+    twin = me + 1 - 2 * lax.rem(me, 2)
+
+    def slope_copy(peer, owner):
+        return pltpu.make_async_remote_copy(
+            src_ref=slope_ref.at[owner],
+            dst_ref=slope_ref.at[owner],
+            send_sem=slope_send.at[peer, owner],
+            recv_sem=slope_recv.at[owner],
+            device_id=(peer, t_me),
+            device_id_type=MESH,
+        )
+
+    for step in range(2, n_dp, 2):
+        slope_copy(lax.rem(me + step, n_dp), me).start()
+    slope_copy(twin, me).start()
+
+    psi_box[t_me] = lax.dot_general(
+        head_ref[...],
+        act_ref[...],
+        (((1,), (1,)), ((), ())),
+        precision=lax.Precision.HIGHEST,
+        preferred_element_type=jnp.float32,
+    )
+
+    def psi_copy(peer, source):
+        return pltpu.make_async_remote_copy(
+            src_ref=psi_box.at[t_me],
+            dst_ref=psi_box.at[source],
+            send_sem=psi_send.at[peer],
+            recv_sem=psi_recv.at[source],
+            device_id=(me, peer),
+            device_id_type=MESH,
+        )
+
+    for step in range(1, n):
+        psi_copy(lax.rem(t_me + step, n), t_me).start()
+    for step in range(1, n):
+        t = lax.rem(t_me + step, n)
+        psi_copy(t, t).wait_recv()
+    total = psi_box[0]
+    for t in range(1, n):
+        total = total + psi_box[t]
+    psi_ref[...] = total
+
+    for step in range(2, n_dp, 2):
+        peer = lax.rem(me + step, n_dp)
+        slope_copy(peer, peer).wait_recv()
+        slope_copy(twin, peer).start()
+    slope_copy(twin, twin).wait_recv()
+    for step in range(2, n_dp, 2):
+        peer = lax.rem(twin + step, n_dp)
+        slope_copy(twin, peer).wait_recv()
+
+    for step in range(2, n_dp, 2):
+        peer = lax.rem(me + step, n_dp)
+        slope_copy(peer, me).wait_send()
+        slope_copy(twin, peer).wait_send()
+    slope_copy(twin, me).wait_send()
+    for step in range(1, n):
+        psi_copy(lax.rem(t_me + step, n), t_me).wait_send()
+    for step in range(1, n_dp):
+        peer = lax.rem(me + step, n_dp)
+        meta_copy(peer, me).wait_send()
+        meta_copy(peer, peer).wait_recv()
 
     for step in range(1, n_dp):
         peer = lax.rem(me + step, n_dp)
@@ -202,47 +298,67 @@
         for way in range(2):
             for q in range(PIECES):
                 sum_copy(way, q, step, True).wait_send()
-            ring_copy(way, step).wait_send()
+            for i in range(half):
+                ring_copy(way, step, i).wait_send()
         return carry
 
     lax.fori_loop(0, n - 1, finish, 0)
 
 
-def ring_call(n_dp, n, part, resid, gain, twist):
+def ring_call(n_dp, n, part, resid, gain, twist, head, meta):
     rows, width = resid.shape
     feats, units = twist.shape
     half, per = n_dp // 2, n // n_dp
+    span = per * n_dp * rows
     piece = width // (2 * PIECES)
     dma = pltpu.SemaphoreType.DMA
     vmem = pl.BlockSpec(memory_space=pltpu.VMEM)
-    pre_act, columns = pl.pallas_call(
+    active, columns, slope, psi, metas = pl.pallas_call(
         functools.partial(ring_kernel, n_dp, n),
         out_shape=(
-            jax.ShapeDtypeStruct((per, 2, half * rows, units), jnp.float32),
+            jax.ShapeDtypeStruct((span, units), jnp.float32),
             jax.ShapeDtypeStruct((n, n_dp, rows, feats), jnp.bfloat16),
+            jax.ShapeDtypeStruct((n_dp, per, 2, half * rows, units), jnp.bfloat16),
+            jax.ShapeDtypeStruct((8, span), jnp.float32),
+            jax.ShapeDtypeStruct((n_dp,) + meta.shape, jnp.int32),
         ),
-        in_specs=[vmem] * 4,
-        out_specs=(vmem, vmem),
+        in_specs=[vmem] * 6,
+        out_specs=(vmem,) * 5,
         scratch_shapes=[
             pltpu.VMEM((2, PIECES, n - 1, rows, piece), jnp.bfloat16),
             pltpu.VMEM((rows, width), jnp.bfloat16),
             pltpu.VMEM((n_dp, rows, feats), jnp.bfloat16),
             pltpu.VMEM((n, 2, half * rows, units), jnp.bfloat16),
             pltpu.VMEM((n_dp, per, 2, half * rows, units), jnp.bfloat16),
+            pltpu.VMEM((n, 8, span), jnp.float32),
             dma((2, PIECES, n - 1)),
             dma((2, PIECES, n - 1)),
             dma((n_dp,)),
             dma((n_dp,)),
-            dma((2, n - 1)),
-            dma((2, n - 1)),
+            dma((2, n - 1, half)),
+            dma((2, n - 1, half)),
             dma((n, 2)),
             dma((n_dp, per, 2)),
+            dma((n_dp,)),
+            dma((n_dp,)),
+            dma((n_dp, n_dp)),
+            dma((n_dp,)),
+            dma((n,)),
+            dma((n,)),
         ],
         compiler_params=pltpu.CompilerParams(
             collective_id=0, has_side_effects=True, vmem_limit_bytes=44 * 1024 * 1024
         ),
-    )(part.reshape(n, rows, width), resid, gain.reshape(1, width), twist)
-    return pre_act.reshape(per * n_dp * rows, units), columns.reshape(n * n_dp * rows, feats)
+    )(
+        part.reshape(n, rows, width),
+        resid,
+        gain.reshape(1, width),
+        twist,
+        jnp.broadcast_to(head[None, :], (8, units)),
+        meta,
+    )
+    columns = columns.reshape(n * n_dp * rows, feats)
+    return active, columns, slope.reshape(n_dp * span, units), psi[0], metas.reshape(n_dp, -1)
 
 
 def make_local(n_dp, n_tensor):
@@ -264,26 +380,27 @@
         tokens = seq_len * n_dp
         me = lax.axis_index("dp")
 
-        ids_all = lax.all_gather(
-            jnp.concatenate([token_ids, toxicity, prompt_len]), "dp", axis=0
-        )
-        levels_all = ids_all[:, seq_len].astype(jnp.float32)
-        prompt_all = ids_all[:, seq_len + 1]
-        ids_all = ids_all[:, :seq_len]
+        meta = jnp.concatenate([token_ids, toxicity, prompt_len])
+        meta = jnp.pad(meta, (0, -meta.shape[0] % 1024)).reshape(-1, 128)
 
         partial_sum = jnp.dot(attn_heads, out_proj, preferred_element_type=jnp.float32)
-        pre_act, columns = ring_call(
-            n_dp, n_tensor, partial_sum.astype(jnp.bfloat16), residual, norm_gain, twist_in
-        )
-        sigma = jax.nn.sigmoid(pre_act)
-        active = pre_act * sigma
-        slope = (twist_out[None, :] * sigma * (1.0 + pre_act * (1.0 - sigma))).astype(jnp.bfloat16)
-        slope_all = lax.all_gather(slope, "dp", axis=0, tiled=True)
+        active, columns, slope_all, psi, metas = ring_call(
+            n_dp,
+            n_tensor,
+            partial_sum.astype(jnp.bfloat16),
+            residual,
+            norm_gain,
+            twist_in,
+            twist_out,
+            meta,
+        )
+        levels_all = metas[:, seq_len].astype(jnp.float32)
+        prompt_all = metas[:, seq_len + 1]
+        ids_all = metas[:, :seq_len]
 
         span = seq_len // n_dp
         blocks = span // rows
         own_ids = lax.dynamic_slice_in_dim(ids_all, me * span, span, axis=1)
-        psi = lax.psum(jnp.sum(active * twist_out[None, :], axis=1), "tensor")
         grid = psi.reshape(blocks, n_dp, rows).transpose(1, 0, 2).reshape(n_dp, span)
         grid = grid + token_bias[own_ids]
         live = (me * span + jnp.arange(span))[None, :] >= prompt_all[:, None]
@@ -311,8 +428,13 @@
         own_vocab = vocab_size // n_dp
         ids_perm = ids_all.reshape(n_dp, n_tensor, rows).transpose(1, 0, 2).reshape(-1)
         spot = ids_perm - me * own_vocab
-        spot = jnp.where((spot >= 0) & (spot < own_vocab), spot, own_vocab)
-        grad_bias = jnp.zeros((own_vocab,), jnp.float32).at[spot].add(flat_all, mode="drop")
+        lines = -(-own_vocab // 128)
+        inside = (spot >= 0) & (spot < own_vocab)
+        line = jnp.where(inside, spot // 128, -1)
+        high = jnp.where(jnp.arange(lines)[:, None] == line[None, :], flat_all[None, :], 0.0)
+        low = (jnp.arange(128)[None, :] == (spot % 128)[:, None]).astype(jnp.float32)
+        grad_bias = jnp.dot(high, low, precision=lax.Precision.HIGHEST)
+        grad_bias = grad_bias.reshape(-1)[:own_vocab]
         return (twist_vals, grad_in, grad_out, grad_bias)
 
     return local

time: 193 us -> 161 us (0.83)
  blocking collectives: 27.8 us -> 5.21 us
  between operations: 16.2 us -> 2.07 us
  Pallas kernels: 111 us -> 121 us
  other arithmetic: 9.88 us -> 3.06 us
  local copies, waits for them, and re-layouts: 7.04 us -> 9.3 us
    psum x1 -> x0, blocking collectives: 18.3 us -> none  [local(): psi = lax.psum(jnp.sum(active * twist_out[None, :], axis=1), 'tensor')]
    pallas_call x1, Pallas kernels: 111 us -> 121 us  [ring_call(): pl.pallas_call(functools.partial(ring_kernel, n_dp, n), out_shape=(jax.Sh...]
    scatter-add x1 -> x0, other arithmetic: 6.71 us -> none  [local(): jnp.zeros((own_vocab,), jnp.float32).at[spot].add(flat_all, mode='drop')]
    unnamed x1 -> x0, blocking collectives: 4.31 us -> none
    dot_general x1, matrix products: 10.9 us -> 6.91 us  [local(): lax.dot_general(columns, d_pre, contract, preferred_element_type=jnp.floa...]
    unnamed x22 -> x23, local copies, waits for them, and re-layouts: 3.53 us -> 5.85 us
  transfers between devices with their start and end apart: 1 -> 0, of which waited for: 0 -> 0; matrix products, arithmetic and copies ran while one was open for 7% -> 0% of each run, Pallas kernels for 0% -> 0%
where the time goes in v3:
time: 161 us
  Pallas kernels  121 us (75%)
  matrix products  20.2 us (13%)
  local copies, waits for them, and re-layouts  9.3 us (6%)
  blocking collectives  5.21 us (3%)
  other arithmetic  3.06 us (2%)
  between operations  2.07 us (1%)
    pallas_call x1, Pallas kernels, ring_call(): pl.pallas_call(functools.partial(ring_kernel, n_dp, n), out_shape=(jax.Sh...  121 us
    dot_general x1, matrix products, local(): jnp.dot(attn_heads, out_proj, preferred_element_type=jnp.float32)  11.8 us
    dot_general x1, matrix products, local(): lax.dot_general(columns, d_pre, contract, preferred_element_type=jnp.floa...  6.91 us
    unnamed x23, local copies, waits for them, and re-layouts  5.85 us
    all_gather x1, blocking collectives, local(): packed = lax.all_gather(packed, 'dp', axis=0)  5.21 us

profile of v3, /device:TPU:0, one launch (start us, length us, event | category | flops | bytes accessed | tf_op | source)
XLA Modules:
  0.0 160.5 jit_solution(7079834370517109094)
XLA Ops:
  0.6 0.0 copy-start
  0.6 0.0 copy-start.2
  0.7 0.0 copy-start.3
  0.7 0.0 copy-start.7
  0.7 0.0 copy-start.8
  0.7 1.0 copy-done
  1.7 11.8 %convolution_convert_fusion = bf16[256,8192]{1,0:T(8,128)(2,1)} fusion(bf16[256,1024]{1,0:T(8,128)(2,1)S(1)} %copy-done, bf16[1024,8192]{1,0:T(8,128)(2,1)} %param.12), kind=kOutput, calls=%fused_computation.1 | convolution fusion | flops 4297064448 | bytes 21495808 | tf_op jit(solution)/shard_map/dot_general | solution.py:386
  13.5 0.0 copy-done.7
  14.8 0.0 copy-done.8
  14.8 0.1 pad_add_fusion
  14.9 0.0 copy-done.2
  14.9 0.0 copy-done.3
  14.9 0.0 copy-start.6
  14.9 120.7 %shard_map.129 = (f32[256,1024]{1,0:T(8,128)S(1)}, bf16[8,4,32,2048]{3,2,1,0:T(8,128)(2,1)S(1)}, bf16[4,2,2,64,1024]{4,3,2,1,0:T(8,128)(2,1)S(1)}, f32[8,256]{1,0:T(8,128)S(1)}, s32[4,8,128]{2,1,0:T(8,128)S(1)}) custom-call(bf16[8,32,8192]{2,1,0:T(8,128)(2,1)} %bitcast.39, bf16[32,8192]{1,0:T(8,128)(2,1)S(1)} %copy-done.2, f32[1,8192]{1,0:T(1,128)S(1)} %bitcast.36, ...), custom_call_target="tpu_custom_call" | custom-call | tf_op jit(solution)/shard_map/pallas_call | solution.py:316
  135.7 0.0 copy-start.1
  135.7 1.0 copy-done.1
  136.7 0.0 copy-start.4
  136.7 2.0 %copy-done.4 = bf16[8,4,32,2048]{3,2,1,0:T(8,128)(2,1)} copy-done((bf16[8,4,32,2048]{3,2,1,0:T(8,128)(2,1)}, bf16[8,4,32,2048]{3,2,1,0:T(8,128)(2,1)S(1)}, u32[]{:S(2)}) %copy-start.4) | copy-done | bytes 4194328
  138.7 0.2 slice_reduce_fusion.1
  138.9 0.1 compare_select_fusion.4
  139.0 0.1 reshape.190
  139.0 0.0 copy-done.6
  139.1 1.7 %gather_fusion = f32[256]{0:T(256)S(1)} fusion(f32[128256]{0:T(1024)S(1)} %copy-done.6, s32[1024]{0:T(1024)S(1)} %pad_clamp_fusion), kind=kCustom, calls=%fused_computation | custom fusion | bytes 3072 | tf_op jit(solution)/shard_map/gather | solution.py:405
  140.8 0.1 gather.8
  140.9 0.1 reshape_squeeze.3
  141.0 0.1 fusion.6
  141.1 0.1 fusion.15
  141.1 0.1 fusion.12
  141.3 0.1 select_reduce_fusion
  141.4 0.1 max.19
  141.5 0.1 fusion.9
  141.5 0.1 reshape.182
  141.6 1.4 multiply_reduce_fusion
  143.0 0.1 reshape.183
  143.1 5.2 %all-gather.1 = f32[4,1,1536]{2,1,0:T(1,128)S(1)} all-gather(f32[1,1,1536]{2,1,0:T(1,128)S(1)} %reshape.201), channel_id=2, replica_groups=mesh['dp'=4,'tensor'=8] {'dp'}, dimensions={0}, use_global_device_ids=true | all-gather | bytes 30720 | tf_op jit(solution)/shard_map/all_gather | solution.py:418
  148.4 0.1 reshape.184
  148.5 0.6 reshape.185
  149.1 0.1 mul.48
  149.2 0.0 copy-start.5
  149.2 0.4 multiply_convert_fusion
  149.6 1.8 %copy-done.5 = bf16[8,4,32,2048]{3,2,1,0:T(8,128)(2,1)S(1)} copy-done((bf16[8,4,32,2048]{3,2,1,0:T(8,128)(2,1)S(1)}, bf16[8,4,32,2048]{3,2,1,0:T(8,128)(2,1)}, u32[]{:S(2)}) %copy-start.5) | copy-done | bytes 4194328
  151.4 6.9 %fusion.16 = f32[2048,1024]{1,0:T(8,128)} fusion(bf16[1024,2048]{1,0:T(8,128)(2,1)S(1)} %bitcast.38, bf16[1024,1024]{1,0:T(8,128)(2,1)S(1)} %bitcast.40), kind=kOutput, calls=%fused_computation.54 | convolution fusion | flops 4294967296 | bytes 14680064 | tf_op jit(solution)/shard_map/dot_general | solution.py:426
  158.3 0.6 slice_reduce_fusion
  158.9 0.1 sub.48
  159.0 0.1 sub.50
  159.1 1.5 convolution_bitcast_fusion
  (21 shorter events, 0.2 us)
Async XLA Ops:
  0.6 1.1 copy-start
  0.6 14.3 %copy-start.2 = (bf16[32,8192]{1,0:T(8,128)(2,1)S(1)}, bf16[32,8192]{1,0:T(8,128)(2,1)}, u32[]{:S(2)}) copy-start(bf16[32,8192]{1,0:T(8,128)(2,1)} %resid_ref.1) | copy-start | bytes 1572868
  0.7 14.3 %copy-start.3 = (f32[8192]{0:T(1024)S(1)}, f32[8192]{0:T(1024)}, u32[]{:S(2)}) copy-start(f32[8192]{0:T(1024)} %param.14) | copy-start | bytes 98308
  0.7 12.9 %copy-start.7 = (f32[1024]{0:T(1024)S(1)}, f32[1024]{0:T(1024)}, u32[]{:S(2)}) copy-start(f32[1024]{0:T(1024)} %param.16) | copy-start | bytes 12292
  0.7 14.2 %copy-start.8 = (s32[256]{0:T(256)S(1)}, s32[256]{0:T(256)}, u32[]{:S(2)}) copy-start(s32[256]{0:T(256)} %param.10) | copy-start | bytes 3076
  14.9 124.1 %copy-start.6 = (f32[128256]{0:T(1024)S(1)}, f32[128256]{0:T(1024)}, u32[]{:S(2)}) copy-start(f32[128256]{0:T(1024)} %param.17) | copy-start | bytes 1539076
  135.7 1.0 copy-start.1
  136.7 2.0 %copy-start.4 = (bf16[8,4,32,2048]{3,2,1,0:T(8,128)(2,1)}, bf16[8,4,32,2048]{3,2,1,0:T(8,128)(2,1)S(1)}, u32[]{:S(2)}) copy-start(bf16[8,4,32,2048]{3,2,1,0:T(8,128)(2,1)S(1)} %get-tuple-element.12) | copy-start | bytes 12582916
  149.2 2.2 %copy-start.5 = (bf16[8,4,32,2048]{3,2,1,0:T(8,128)(2,1)S(1)}, bf16[8,4,32,2048]{3,2,1,0:T(8,128)(2,1)}, u32[]{:S(2)}) copy-start(bf16[8,4,32,2048]{3,2,1,0:T(8,128)(2,1)} %copy-done.4) | copy-start | bytes 12582916
